TPU v7x, 768 devices: a whole 4x8x12 slice. The times are simulated.
768 devices in a mesh: row: 6 (over z_hi, core), col: 128 (over z_lo, x, y).
Axes of the slice: x: 4, y: 8, z: 12 (z_hi: 3, z_lo: 4; z = z_hi * 4 + z_lo), core: 2. Of those that a mesh axis runs over, the one named last changes fastest.
Arguments:
- tokens: bfloat16 [816, 8192], P('row', 'col'), may hold values from -6 to 6
- w_in: bfloat16 [8192, 24576], P(None, 'col'), may hold values from -0.0625 to 0.0625
- short_filter: float32 [3, 24576], P(None, 'col'), may hold values from -3.5 to 3.5
- mr_filter: float32 [512, 128], P('col'), may hold values from -0.5 to 0.5
- skip: float32 [8192], P('col'), may hold values from 0.5 to 1.5
- w_out: bfloat16 [8192, 8192], P(None, 'col'), may hold values from -0.0625 to 0.0625
- grad_out: bfloat16 [816, 8192], P('row', 'col'), may hold values from -0.119628906 to 0.119628906
Outputs:
- block_out: bfloat16 [816, 8192], P('row', 'col')
- filter_grad: float32 [512, 128], P('col')
- skip_grad: float32 [8192], P('col')
All inputs are finite; a program needn't handle non-finite values.
Results may differ from a plain program's by a relative error of at most 0.0085.
Values may be sent and summed in bfloat16 or wider, within the bound.
A program may use at most 64 MiB of HBM per device.

v0:
```python
import jax
import jax.numpy as jnp
from jax import lax
from jax.sharding import PartitionSpec as P


def passed_along(block, axis, distance):
    devices = range(lax.axis_size(axis))
    route = [(i - distance, i) for i in devices if i - distance in devices]
    return lax.ppermute(block, axis, route)


def local(tokens, w_in, short_filter, mr_filter, skip, w_out, grad_out):
    row_count = tokens.shape[0]
    local_width = tokens.shape[1]
    group_count = mr_filter.shape[0]
    group_width = local_width // group_count
    tap_count = mr_filter.shape[1]
    span_rows = row_count + tap_count - 1
    highest = lax.Precision.HIGHEST
    weight_rows = w_in
    proj_sum = jnp.dot(
        lax.all_gather(tokens, "col", axis=1, tiled=True),
        weight_rows,
        preferred_element_type=jnp.float32,
    )
    projected = proj_sum.astype(jnp.bfloat16)
    earlier = passed_along(projected[row_count - tap_count - 1 :], "row", 1)
    extended = jnp.concatenate([earlier, projected], 0).astype(jnp.float32)
    short_rows = (
        short_filter[0] * extended[2:]
        + short_filter[1] * extended[1:-1]
        + short_filter[2] * extended[:-2]
    )
    branches = short_rows.reshape(short_rows.shape[0], group_count, 3, group_width)
    query_all = branches[:, :, 0, :]
    mixed_ext = branches[:, :, 1, :] * branches[:, :, 2, :]
    query = query_all[tap_count - 1 :]
    mixed_own = mixed_ext[tap_count - 1 :]
    reversed_taps = mr_filter[:, ::-1]
    tap_vector = jnp.concatenate(
        [reversed_taps, jnp.zeros((group_count, row_count), jnp.float32)], 1
    )
    toeplitz = jnp.tile(tap_vector, (1, row_count))[:, : row_count * span_rows].reshape(
        group_count, row_count, span_rows
    )
    longconv = jnp.einsum("gts,sgi->tgi", toeplitz, mixed_ext, precision=highest)
    skip_table = skip.reshape(group_count, group_width)
    gated = (
        (query * (longconv + skip_table * mixed_own))
        .astype(jnp.bfloat16)
        .reshape(row_count, local_width)
    )
    weight_rows = w_out
    out_sum = jnp.dot(
        lax.all_gather(gated, "col", axis=1, tiled=True),
        weight_rows,
        preferred_element_type=jnp.float32,
    )
    block_out = out_sum.astype(jnp.bfloat16)
    weight_rows = w_out
    grad_cols = lax.psum_scatter(
        lax.dot_general(
            weight_rows, grad_out, (((1,), (1,)), ((), ())), preferred_element_type=jnp.float32
        ),
        "col",
        scatter_dimension=0,
        tiled=True,
    ).T
    weighted = grad_cols.reshape(row_count, group_count, group_width) * query
    correlation = jnp.einsum("tgi,sgi->gts", weighted, mixed_ext, precision=highest)
    flattened = jnp.pad(
        correlation.reshape(group_count, row_count * span_rows), ((0, 0), (0, row_count))
    )
    diagonals = flattened.reshape(group_count, row_count, span_rows + 1)[:, :, :tap_count]
    tap_part = jnp.sum(diagonals, axis=1)[:, ::-1]
    skip_part = jnp.sum(weighted * mixed_own, axis=0).reshape(local_width)
    filter_grad, skip_grad = lax.psum((tap_part, skip_part), "row")
    return (block_out, filter_grad, skip_grad)


def solution(mesh):
    in_specs = (
        P("row", "col"),
        P(None, "col"),
        P(None, "col"),
        P("col", None),
        P("col"),
        P(None, "col"),
        P("row", "col"),
    )
    out_specs = (P("row", "col"), P("col", None), P("col"))
    return jax.shard_map(local, mesh=mesh, in_specs=in_specs, out_specs=out_specs, check_vma=False)
```

profile of v0, /device:TPU:1, one launch (start us, length us, event | category | flops | bytes accessed | tf_op | source)
XLA Modules:
  0.0 2212.5 jit_solution(9617261892061138610)
XLA Ops:
  7.2 0.0 copy-start
  7.2 0.0 copy-start.1
  7.2 0.0 copy-start.2
  7.2 0.0 all-gather.3.cloned.1.call-start
  7.2 0.7 all-gather.3.cloned.1.call-update
  7.9 0.0 all-gather.5.cloned.1.call-start
  8.0 618.9 %all-gather.3.cloned.1.call-done = bf16[136,8192]{0,1:T(8,128)(2,1)} async-done(((bf16[136,64]{0,1:T(8,128)(2,1)}), bf16[136,8192]{0,1:T(8,128)(2,1)}) %all-gather.3.cloned.1.call-update) | async-done | bytes 2228240 | tf_op jit(solution)/shard_map/all_gather | solution.py:23
  626.9 0.0 copy-done
  626.9 3.6 convolution_convert_fusion
  630.5 0.0 copy-start.3
  630.6 95.9 %collective-permute-start = (bf16[129,192]{1,0:T(8,128)(2,1)S(1)}, bf16[129,192]{1,0:T(8,128)(2,1)S(1)}, u32[]{:S(2)}, u32[]{:S(2)}) collective-permute-start(bf16[129,192]{1,0:T(8,128)(2,1)S(1)} %slice.62), channel_id=1, source_target_pairs={{0,128},{128,256},{256,384},{384,512},{512,640},{1,129},{129,257},... | collective-permute-start | bytes 148616 | tf_op jit(solution)/shard_map/ppermute | solution.py:10
  726.5 0.0 copy-done.1
  726.5 0.0 copy-done.2
  726.5 0.1 rev.6
  726.6 1.0 tile.4
  727.6 2.5 tile.10
  730.1 1.9 slice.69
  732.0 2.6 reshape.36
  734.6 0.0 copy-done.3
  734.6 0.1 mul.66
  734.7 0.0 collective-permute-done
  734.7 0.8 fusion.3
  735.5 1.1 copy.13
  736.6 2.8 fusion.2
  739.4 0.0 all-gather.5.cloned.1.call-update
  739.4 0.0 reduce-scatter.2.cloned.1.call-start
  739.5 5.7 fusion.12
  745.2 0.0 reduce-scatter.2.cloned.1.call-update
  745.2 592.6 %all-gather.5.cloned.1.call-done = bf16[136,8192]{0,1:T(8,128)(2,1)} async-done(((bf16[136,64]{0,1:T(8,128)(2,1)}), bf16[136,8192]{0,1:T(8,128)(2,1)}) %all-gather.5.cloned.1.call-update) | async-done | bytes 2228240 | tf_op jit(solution)/shard_map/all_gather | solution.py:56
  1337.8 3.9 convolution_convert_fusion.1
  1341.8 734.7 %reduce-scatter.2.cloned.1.call-done = f32[64,136]{1,0:T(8,128)} async-done(((f32[8192,136]{1,0:T(8,128)}), f32[64,136]{1,0:T(8,128)}) %reduce-scatter.2.cloned.1.call-update) | async-done | bytes 34832 | tf_op jit(solution)/shard_map/reduce_scatter | solution.py:62
  2076.5 3.0 fusion.6
  2079.5 1.0 multiply_reduce_fusion
  2080.6 2.6 reshape.39
  2083.1 2.0 pad.5
  2085.1 2.5 reshape.40
  2087.6 1.0 slice_reduce_fusion
  2088.6 0.1 rev.7
  2088.7 0.1 reshape.41
  2088.8 117.2 %all-reduce.2 = (f32[4,128]{1,0:T(4,128)}, f32[64]{0:T(128)}) all-reduce(f32[4,128]{1,0:T(4,128)S(1)} %rev.7, f32[64]{0:T(128)S(1)} %reshape.41), channel_id=1, replica_groups=mesh['row'=6,'col'=128] {'row'}, use_global_device_ids=true, to_apply=%region_2.3 | all-reduce | flops 576 | bytes 4608 | tf_op jit(solution)/shard_map/psum | solution.py:78
  (5 shorter events, 0.1 us)
Async XLA Ops:
  7.2 619.7 %copy-start = (bf16[8192,192]{0,1:T(8,128)(2,1)S(1)}, bf16[8192,192]{0,1:T(8,128)(2,1)}, u32[]{:S(2)}) copy-start(bf16[8192,192]{0,1:T(8,128)(2,1)} %param.8) | copy-start | bytes 9437188
  7.2 719.3 %copy-start.1 = (f32[3,192]{1,0:T(4,128)S(1)}, f32[3,192]{1,0:T(4,128)}, u32[]{:S(2)}) copy-start(f32[3,192]{1,0:T(4,128)} %param.9) | copy-start | bytes 6916
  7.2 719.3 %copy-start.2 = (f32[4,128]{1,0:T(4,128)S(1)}, f32[4,128]{1,0:T(4,128)}, u32[]{:S(2)}) copy-start(f32[4,128]{1,0:T(4,128)} %param.10) | copy-start | bytes 6148
  7.2 619.7 %all-gather.3.cloned.1.call-start = ((), (), s32[]{:S(2)}) async-start(), calls=%async_computation.1 | async-start | bytes 4227072 | tf_op jit(solution)/shard_map/all_gather | solution.py:23
  7.9 1329.9 %all-gather.5.cloned.1.call-start = ((), (), s32[]{:S(2)}) async-start(), calls=%async_computation.2 | async-start | bytes 4227072 | tf_op jit(solution)/shard_map/all_gather | solution.py:56
  630.5 104.1 %copy-start.3 = (f32[64]{0:T(128)S(1)}, f32[64]{0:T(128)}, u32[]{:S(2)}) copy-start(f32[64]{0:T(128)} %param.11) | copy-start | bytes 772
  630.6 104.1 %collective-permute-start = (bf16[129,192]{1,0:T(8,128)(2,1)S(1)}, bf16[129,192]{1,0:T(8,128)(2,1)S(1)}, u32[]{:S(2)}, u32[]{:S(2)}) collective-permute-start(bf16[129,192]{1,0:T(8,128)(2,1)S(1)} %slice.62), channel_id=1, source_target_pairs={{0,128},{128,256},{256,384},{384,512},{512,640},{1,129},{129,257},... | collective-permute-start | bytes 148616 | tf_op jit(solution)/shard_map/ppermute | solution.py:10
  739.4 1337.1 %reduce-scatter.2.cloned.1.call-start = ((), (), s32[]{:S(2)}) async-start(), calls=%async_computation.3 | async-start | bytes 8454144 | tf_op jit(solution)/shard_map/reduce_scatter | solution.py:62
Sparse Core Ops, SparseCore 0:
  10.4 616.4 all-gather.2
  739.5 598.2 all-gather.4
  1340.9 735.5 reduce-scatter.1
where the time goes:
time: 2210 us
  waiting for transfers between devices  1950 us (88%)
  blocking collectives  117 us (5%)
  starting transfers between devices  96.1 us (4%)
    reduce_scatter x1, waiting for transfers between devices, local(): lax.psum_scatter(lax.dot_general(weight_rows, grad_out, (((1,), (1,)), ((...  735 us
    all_gather x1, waiting for transfers between devices, local(): lax.all_gather(tokens, 'col', axis=1, tiled=True)  619 us
    all_gather x1, waiting for transfers between devices, local(): lax.all_gather(gated, 'col', axis=1, tiled=True)  593 us
    psum x1, blocking collectives, local(): filter_grad, skip_grad = lax.psum((tap_part, skip_part), 'row')  117 us
    ppermute x1, starting transfers between devices, passed_along(): return lax.ppermute(block, axis, route)  95.9 us
  transfers between devices with their start and end apart: 4, of which 3 were waited for; matrix products, arithmetic and copies ran while one was open for 1% of the time, Pallas kernels for 0%

commit v1 on v0

v1 whole, which is shorter than its diff:
```python
import jax
import jax.numpy as jnp
from jax import lax
from jax.experimental import pallas as pl
from jax.experimental.pallas import tpu as pltpu
from jax.sharding import PartitionSpec as P

MESH = pl.DeviceIdType.MESH
NX, NY, NZ, NR = 4, 8, 4, 6
NP = NX * NY
ROWS = 136
PAD = 144
CUT = 80
CUT2 = 64
TAPS = 128
WIDE = 384
BF = jnp.bfloat16
F32 = jnp.float32
HIGH = lax.Precision.HIGHEST
NSEM = 160


class Comm:
    def __init__(self, ss, rs):
        self.ss, self.rs, self.count, self.started = ss, rs, 0, []

    def send(self, src, dst, dev):
        i = self.count
        self.count += 1
        copy = pltpu.make_async_remote_copy(
            src_ref=src,
            dst_ref=dst,
            send_sem=self.ss.at[i],
            recv_sem=self.rs.at[i],
            device_id=dev,
            device_id_type=MESH,
        )
        copy.start()
        self.started.append(copy)
        return (i, dev)

    def arrive(self, handle, dst):
        i, dev = handle
        pltpu.make_async_remote_copy(
            src_ref=dst,
            dst_ref=dst,
            send_sem=self.ss.at[i],
            recv_sem=self.rs.at[i],
            device_id=dev,
            device_id_type=MESH,
        ).wait_recv()

    def finish(self):
        for copy in self.started:
            copy.wait_send()


def iota(shape, dim):
    return lax.broadcasted_iota(jnp.int32, shape, dim)


def swap(v):
    return pltpu.roll(v, 64, 1)


def low(v):
    return iota(v.shape, 1) < 64


def lows(a, b):
    return jnp.where(low(a), a, swap(b))


def highs(a, b):
    return jnp.where(low(a), swap(a), b)


def pack(tile, half):
    top = tile[:CUT]
    rest = jnp.concatenate([tile[CUT:], jnp.zeros((2 * CUT - PAD, 128), F32)], 0)
    return lows(top, rest) if half == 0 else highs(top, rest)


def unpack(v):
    up = swap(v)
    full = jnp.concatenate([v, up[: PAD - CUT]], 0)
    return jnp.where(low(full), full, 0.0)


def dot(a, b):
    return jnp.dot(a, b, preferred_element_type=F32)


def dot_t(a, b):
    return lax.dot_general(a, b, (((1,), (1,)), ((), ())), preferred_element_type=F32)


def kernel(
    tok, grd, win, sfl, flt, skp, wout,
    out_ref, fg_ref, sg_ref,
    wv, wov, zr, gath, wpk, wrv, wz, acc, gz, gp, gr, yp, yr, hs, hr, pb, h2r, gated, op, orv, pr, toep,
    ss, rs, ls,
):
    r = lax.axis_index("row")
    c = lax.axis_index("col")
    core = r % 2
    z = c // NP
    x = (c // NY) % NX
    y = c % NY
    sgn = 1 - 2 * core
    comm = Comm(ss, rs)

    def at(dx=0, dy=0, dz=0):
        return (r, ((z + dz + NZ) % NZ) * NP + ((x + dx + NX) % NX) * NY + (y + dy + NY) % NY)

    def chunk(dx, dy):
        return ((x - dx + NX) % NX) * NY + (y - dy + NY) % NY

    def by_row(i):
        return ((r + i) % NR, c)

    sibling = (r + sgn, c)
    own = chunk(0, 0)

    loads = [pltpu.make_async_copy(wout, wov, ls.at[0])]
    for k in range(NZ):
        loads.append(pltpu.make_async_copy(win.at[k], wv.at[:, pl.ds(64 * k, 64), :], ls.at[1 + k]))
    for load in loads:
        load.start()

    peers = [at(dz=i) for i in range(1, NZ)] + [at(dx=i) for i in range(1, NX)]
    peers += [at(dy=i) for i in range(1, NY)] + [by_row(i) for i in range(1, NR)]
    barrier = pltpu.get_barrier_semaphore()
    for peer in peers:
        pl.semaphore_signal(barrier, inc=1, device_id=peer, device_id_type=MESH)

    both = jnp.concatenate([tok[...].astype(F32), grd[...].astype(F32)], 1)
    zr[z] = jnp.concatenate([both, jnp.zeros((PAD - ROWS, 128), F32)], 0).astype(BF)

    pl.semaphore_wait(barrier, len(peers))

    z_moves = [comm.send(zr.at[z], zr.at[z], at(dz=i)) for i in (1, 2, 3)]

    loads[0].wait()
    half = pl.multiple_of(core * 512, 512)
    w_moves = []
    for i in (1, 2, 3):
        base = pl.multiple_of(((z + i) % NZ) * 2048 + core * 512, 512)
        a = wov[pl.ds(base, 512), :].astype(F32)
        b = wov[pl.ds(base + 1024, 512), :].astype(F32)
        wpk[i - 1] = jnp.concatenate([a, b], 1).astype(BF)
        w_moves.append(comm.send(wpk.at[i - 1], wrv.at[z, pl.ds(half, 512)], at(dz=i)))
    mine = pl.multiple_of(z * 2048, 2048)
    wrv[z] = jnp.concatenate(
        [wov[pl.ds(mine, 1024), :].astype(F32), wov[pl.ds(mine + 1024, 1024), :].astype(F32)], 1
    ).astype(BF)

    col = iota((192, WIDE), 1)
    lane = col & 127
    source = (lane >> 4) * 48 + (col >> 7) * 16 + (lane & 15)
    hit = (iota((192, WIDE), 0) == source) & (lane < 64)
    perm = jnp.where(hit, 1.0, 0.0)
    short_taps = jnp.dot(sfl[...], perm, precision=HIGH, preferred_element_type=F32)
    perm_b = perm.astype(BF)

    place = jnp.where((iota((TAPS, WIDE), 0) + iota((TAPS, WIDE), 1)) % WIDE == 0, 1.0, 0.0).astype(BF)
    taps0 = dot(flt[...].astype(BF), place)
    for g in range(4):
        line = jnp.broadcast_to(taps0[g : g + 1], (PAD, WIDE))
        toep[pl.ds(g * PAD, PAD)] = pltpu.roll(line, 0, 1, stride=1, stride_axis=0).astype(BF)

    for load in loads[1:]:
        load.wait()
    for i, move in zip((1, 2, 3), z_moves):
        comm.arrive(move, zr.at[(z - i + NZ) % NZ])
    q0, q1, q2, q3 = [zr[k].astype(F32) for k in range(NZ)]
    gath[own] = jnp.concatenate([lows(q0, q1), lows(q2, q3)], 1).astype(BF)
    gz[...] = jnp.concatenate([highs(q0, q1), highs(q2, q3)], 1).astype(BF)

    parts = {"A": pl.ds(0, CUT), "B": pl.ds(CUT, PAD - CUT)}
    moves = {}

    def pass_on(part, dx, dy, to_dx, to_dy, step_x, step_y):
        ref = gath.at[chunk(dx, dy), parts[part]]
        moves[part, to_dx, to_dy] = comm.send(ref, ref, at(dx=step_x, dy=step_y))

    def y_steps(part, dx, dy):
        if 0 <= dy <= 2:
            pass_on(part, dx, dy, dx, dy + 1, 0, 1)
        if -2 <= dy <= 0:
            pass_on(part, dx, dy, dx, dy - 1, 0, -1)
        if dy == -3:
            pass_on(part, dx, 3 * sgn, dx, 4, 0, sgn)

    def x_steps(part, dx, dy):
        if dx == 0:
            pass_on(part, 0, dy, 1, dy, 1, 0)
            pass_on(part, 0, dy, -1, dy, -1, 0)
        if dx == -1:
            pass_on(part, sgn, dy, 2, dy, sgn, 0)

    def forward(part, dx, dy):
        if part == "A":
            if dx == 0:
                y_steps(part, 0, dy)
            x_steps(part, dx, dy)
        else:
            if dy == 0:
                x_steps(part, dx, 0)
            y_steps(part, dx, dy)

    order = sorted(
        [(dx, dy) for dx in (0, 1, -1, 2) for dy in (0, 1, -1, 2, -2, 3, -3, 4)],
        key=lambda d: (abs(d[0]) + abs(d[1]), abs(d[0]), -d[0], -d[1]),
    )
    forward("A", 0, 0)
    forward("B", 0, 0)

    def project(places):
        total = None
        for dx, dy in places:
            p = chunk(dx, dy)
            term = dot(gath[p], wv[p])
            total = term if total is None else total + term
        return total

    acc[...] = project([(0, 0)])
    w_back = []
    for hop in range(1, 7):
        places = [d for d in order if abs(d[0]) + abs(d[1]) == hop]
        for dx, dy in places:
            for part in ("A", "B"):
                comm.arrive(moves[part, dx, dy], gath.at[chunk(dx, dy), parts[part]])
                forward(part, dx, dy)
        if hop == 4:
            for i, move in zip((1, 2, 3), w_moves):
                ref = wrv.at[(z - i + NZ) % NZ, pl.ds(half, 512)]
                comm.arrive(move, ref)
                w_back.append(comm.send(ref, ref, sibling))
        acc[...] += project(places)

    proj = dot(acc[...].astype(BF), perm_b)
    pb[...] = proj.astype(BF)
    tail_move = comm.send(pb.at[pl.ds(128, 16)], h2r, by_row(1))
    t = iota((PAD, WIDE), 0)
    one = jnp.where(t >= 1, pltpu.roll(proj, 1, 0), 0.0)
    two = jnp.where(t >= 2, pltpu.roll(proj, 2, 0), 0.0)
    s0, s1, s2 = short_taps[0:1], short_taps[1:2], short_taps[2:3]
    short = s0 * proj + s1 * one + s2 * two
    live = iota((PAD, 128), 0) < ROWS
    mixed = jnp.where(live, short[:, 128:256] * short[:, 256:384], 0.0)
    hs[...] = lows(mixed[8:72], mixed[72:136]).astype(BF)
    halo_move = comm.send(hs, hr, by_row(1))

    other = pl.multiple_of(512 - core * 512, 512)
    for i, move in zip((1, 2, 3), w_back):
        comm.arrive(move, wrv.at[(z - i + NZ) % NZ, pl.ds(other, 512)])

    def build(i, carry):
        at_row = pl.multiple_of(i * 128, 128)
        w0, w1, w2, w3 = [wrv[k, pl.ds(at_row, 128), :].astype(F32) for k in range(NZ)]
        wz[pl.ds(at_row, 128), :] = jnp.concatenate([lows(w0, w1), lows(w2, w3)], 1).astype(BF)
        wz[pl.ds(at_row + 1024, 128), :] = jnp.concatenate([highs(w0, w1), highs(w2, w3)], 1).astype(BF)
        return carry

    lax.fori_loop(0, 8, build, 0)
    for k in range(NX):
        gp[k] = dot_t(gz[...], wz[pl.ds(512 * k, 512), :]).astype(BF)
    gx_moves = [comm.send(gp.at[(x + i) % NX], gr.at[x], at(dx=i)) for i in (1, 3, 2)]

    comm.arrive(tail_move, h2r)
    last = jnp.where(r > 0, h2r[...].astype(F32), 0.0)
    before1, before2 = last[7:8], last[6:7]
    t8 = iota((8, WIDE), 0)
    fix = jnp.where(t8 == 0, s1 * before1 + s2 * before2, jnp.where(t8 == 1, s2 * before1, 0.0))
    short = jnp.concatenate([short[:8] + fix, short[8:]], 0)
    query = short[:, :128]
    mixed = jnp.where(live, short[:, 128:256] * short[:, 256:384], 0.0)
    own_b = jnp.concatenate([mixed, jnp.zeros((256 - PAD, 128), F32)], 0).astype(BF)
    near = dot(toep[:, :256], own_b)
    comm.arrive(halo_move, hr)
    h = jnp.where(r > 0, hr[...].astype(F32), 0.0)
    prev = jnp.concatenate([jnp.where(low(h), h, 0.0), jnp.where(low(h), swap(h), 0.0)], 0)
    prev_b = prev.astype(BF)
    big = near + dot(toep[:, 256:], prev_b)
    group = iota((PAD, 128), 1) >> 4
    conv = jnp.zeros((PAD, 128), F32)
    for g in range(4):
        conv = jnp.where(group == g, big[g * PAD : (g + 1) * PAD], conv)
    skip = jnp.concatenate([skp[...], jnp.zeros((1, 64), F32)], 1)
    value = query * (conv + skip * mixed)
    gated[own] = pack(value, 0).astype(BF)

    parts2 = {"A": pl.ds(0, CUT2), "B": pl.ds(CUT2, CUT - CUT2)}
    moves2 = {}
    ys, xs = (1, 7, 2, 6, 3, 5, 4), (1, 3, 2)

    def direct(part, dx, dy, step_x, step_y):
        ref = gated.at[chunk(dx, dy), parts2[part]]
        moves2[part, dx + step_x, dy + step_y] = comm.send(ref, ref, at(dx=step_x, dy=step_y))

    for dy in ys:
        direct("A", 0, 0, 0, dy)
    for dx in xs:
        direct("B", 0, 0, dx, 0)
        direct("A", 0, 0, dx, 0)
    for dy in ys:
        direct("B", 0, 0, 0, dy)

    total = gp[x].astype(F32)
    for i, move in zip((1, 3, 2), gx_moves):
        comm.arrive(move, gr.at[(x - i + NX) % NX])
        total = total + gr[(x - i + NX) % NX].astype(F32)
    for k in range(NY):
        yp[k] = pack(total[:, 128 * (k // 2) : 128 * (k // 2) + 128], k % 2).astype(BF)

    for dx in xs:
        comm.arrive(moves2["B", dx, 0], gated.at[chunk(dx, 0), parts2["B"]])
        for dy in ys:
            direct("B", dx, 0, 0, dy)
    for dy in ys:
        comm.arrive(moves2["A", 0, dy], gated.at[chunk(0, dy), parts2["A"]])
        for dx in xs:
            direct("A", 0, dy, dx, 0)
    gy_moves = [comm.send(yp.at[(y + i) % NY], yr.at[y], at(dy=i)) for i in ys]

    grad = unpack(yp[y].astype(F32))
    for i, move in zip(ys, gy_moves):
        comm.arrive(move, yr.at[(y - i + NY) % NY])
        grad = grad + unpack(yr[(y - i + NY) % NY].astype(F32))
    weighted = jnp.where(live, grad * query, 0.0)
    skip_part = jnp.sum(weighted * mixed, axis=0, keepdims=True)
    flip = jnp.where(iota((PAD, PAD), 0) + iota((PAD, PAD), 1) == PAD - 1, 1.0, 0.0).astype(BF)
    back = dot(flip, weighted.astype(BF))
    stack = jnp.concatenate([jnp.where(group == g, back, 0.0) for g in range(4)], 0).astype(BF)
    ext = jnp.concatenate([own_b, prev_b], 0)
    corr = dot_t(stack, ext)
    lines = [
        jnp.sum(
            pltpu.roll(corr[g * PAD : (g + 1) * PAD], 0, 1, stride=1, stride_axis=0), axis=0, keepdims=True
        )
        for g in range(4)
    ]
    lines = jnp.concatenate(lines + [jnp.zeros((4, WIDE), F32)], 0)
    pick = jnp.where(iota((WIDE, TAPS), 0) + iota((WIDE, TAPS), 1) == PAD - 1, 1.0, 0.0)
    tap_part = jnp.dot(lines, pick, precision=HIGH, preferred_element_type=F32)
    pr[r] = jnp.where(iota((8, 128), 0) == 4, skip_part, tap_part)
    row_moves = [comm.send(pr.at[r], pr.at[r], by_row(i)) for i in range(1, NR)]

    for dx in xs:
        comm.arrive(moves2["A", dx, 0], gated.at[chunk(dx, 0), parts2["A"]])
    for dy in ys:
        comm.arrive(moves2["B", 0, dy], gated.at[chunk(0, dy), parts2["B"]])
    for dy in ys:
        for dx in xs:
            for part in ("A", "B"):
                comm.arrive(moves2[part, dx, dy], gated.at[chunk(dx, dy), parts2[part]])
    outp = jnp.zeros((PAD, 256), F32)
    for k in range(NP // 4):
        u0, u1, u2, u3 = [gated[4 * k + i].astype(F32) for i in range(4)]
        top = jnp.concatenate([lows(u0, u1), lows(u2, u3)], 1)
        rest = jnp.concatenate([highs(u0, u1), highs(u2, u3)], 1)[: PAD - CUT]
        outp = outp + dot(jnp.concatenate([top, rest], 0).astype(BF), wz[pl.ds(256 * k, 256), :])
    for k in range(NZ):
        op[k] = pack(outp[:, 128 * (k // 2) : 128 * (k // 2) + 128], k % 2).astype(BF)
    o_moves = [comm.send(op.at[(z + i) % NZ], orv.at[z], at(dz=i)) for i in (1, 2, 3)]
    result = op[z].astype(F32)
    for i, move in zip((1, 2, 3), o_moves):
        comm.arrive(move, orv.at[(z - i + NZ) % NZ])
        result = result + orv[(z - i + NZ) % NZ].astype(F32)
    out_ref[...] = unpack(result)[:ROWS, :64].astype(BF)

    for i, move in zip(range(1, NR), row_moves):
        comm.arrive(move, pr.at[(r - i + NR) % NR])
    sums = pr[0]
    for k in range(1, NR):
        sums = sums + pr[k]
    fg_ref[...] = sums[:4]
    sg_ref[...] = sums[4:5, :64]
    comm.finish()
    assert comm.count <= NSEM


def local(tokens, w_in, short_filter, mr_filter, skip, w_out, grad_out):
    vmem = pl.BlockSpec(memory_space=pltpu.VMEM)
    hbm = pl.BlockSpec(memory_space=pl.ANY)
    scratch = [
        pltpu.VMEM((NP, 256, 192), BF),
        pltpu.VMEM((8192, 64), BF),
        pltpu.VMEM((NZ, PAD, 128), BF),
        pltpu.VMEM((NP, PAD, 256), BF),
        pltpu.VMEM((NZ - 1, 512, 128), BF),
        pltpu.VMEM((NZ, 1024, 128), BF),
        pltpu.VMEM((2048, 256), BF),
        pltpu.VMEM((PAD, 192), F32),
        pltpu.VMEM((PAD, 256), BF),
        pltpu.VMEM((NX, PAD, 512), BF),
        pltpu.VMEM((NX, PAD, 512), BF),
        pltpu.VMEM((NY, CUT, 128), BF),
        pltpu.VMEM((NY, CUT, 128), BF),
        pltpu.VMEM((64, 128), BF),
        pltpu.VMEM((64, 128), BF),
        pltpu.VMEM((PAD, WIDE), BF),
        pltpu.VMEM((16, WIDE), BF),
        pltpu.VMEM((NP, CUT, 128), BF),
        pltpu.VMEM((NZ, CUT, 128), BF),
        pltpu.VMEM((NZ, CUT, 128), BF),
        pltpu.VMEM((NR, 8, 128), F32),
        pltpu.VMEM((4 * PAD, WIDE), BF),
        pltpu.SemaphoreType.DMA((NSEM,)),
        pltpu.SemaphoreType.DMA((NSEM,)),
        pltpu.SemaphoreType.DMA((1 + NZ,)),
    ]
    out, taps, gains = pl.pallas_call(
        kernel,
        out_shape=(
            jax.ShapeDtypeStruct((ROWS, 64), BF),
            jax.ShapeDtypeStruct((4, TAPS), F32),
            jax.ShapeDtypeStruct((1, 64), F32),
        ),
        in_specs=[vmem, vmem, hbm, vmem, vmem, vmem, hbm],
        out_specs=(vmem, vmem, vmem),
        scratch_shapes=scratch,
        compiler_params=pltpu.CompilerParams(
            collective_id=0, has_side_effects=True, vmem_limit_bytes=56 * 1024 * 1024
        ),
        name="hyena_block",
    )(tokens, grad_out, w_in.reshape(NZ, NP, 64, 192), short_filter, mr_filter, skip.reshape(1, 64), w_out)
    return out, taps, gains.reshape(64)


def solution(mesh):
    in_specs = (
        P("row", "col"),
        P(None, "col"),
        P(None, "col"),
        P("col", None),
        P("col"),
        P(None, "col"),
        P("row", "col"),
    )
    out_specs = (P("row", "col"), P("col", None), P("col"))
    return jax.shard_map(local, mesh=mesh, in_specs=in_specs, out_specs=out_specs, check_vma=False)
```

time: 2210 us -> 92.8 us (0.04)
  waiting for transfers between devices: 1950 us -> 0 us
  blocking collectives: 117 us -> 0 us
  starting transfers between devices: 96.1 us -> 0 us
  Pallas kernels: 0 us -> 77.7 us
    all_gather x2 -> x0, waiting for transfers between devices: 1210 us -> none  [the longest x1 619 us: local(): lax.all_gather(tokens, 'col', axis=1, tiled=True)]
    reduce_scatter x1 -> x0, waiting for transfers between devices: 735 us -> none  [local(): lax.psum_scatter(lax.dot_general(weight_rows, grad_out, (((1,), (1,)), ((...]
    psum x1 -> x0, blocking collectives: 117 us -> none  [local(): filter_grad, skip_grad = lax.psum((tap_part, skip_part), 'row')]
    ppermute x1 -> x0, starting transfers between devices: 95.9 us -> none  [passed_along(): return lax.ppermute(block, axis, route)]
    pallas_call x0 -> x1, Pallas kernels: none -> 77.7 us  [local(): pl.pallas_call(kernel, out_shape=(jax.ShapeDtypeStruct((ROWS, 64), BF), j...]
  transfers between devices with their start and end apart: 4 -> 0, of which waited for: 3 -> 0; matrix products, arithmetic and copies ran while one was open for 1% -> 0% of each run, Pallas kernels for 0% -> 0%
where the time goes in v1:
time: 92.8 us; the launch traced here: 91.9 us
  Pallas kernels  77.7 us (84%)
  local copies, waits for them, and re-layouts  13.6 us (15%)
    pallas_call x1, Pallas kernels, local(): pl.pallas_call(kernel, out_shape=(jax.ShapeDtypeStruct((ROWS, 64), BF), j...  77.7 us
    unnamed x9, local copies, waits for them, and re-layouts  13.6 us

profile of v1, /device:TPU:1, one launch (start us, length us, event | category | flops | bytes accessed | tf_op | source)
XLA Modules:
  0.0 91.9 jit_solution(16078408694246858797)
XLA Ops:
  0.6 0.0 copy-start
  0.6 1.6 %copy.11.tok = bf16[136,64]{1,0:T(8,128)(2,1)} copy(bf16[136,64]{0,1:T(8,128)(2,1)} %param.7) | data formatting | bytes 34816 | tf_op args[0]
  2.3 1.5 %copy.12.grd = bf16[136,64]{1,0:T(8,128)(2,1)} copy(bf16[136,64]{0,1:T(8,128)(2,1)} %param.13) | data formatting | bytes 34816 | tf_op args[6]
  3.7 2.7 %copy.13.wout = bf16[8192,64]{1,0:T(8,128)(2,1)} copy(bf16[8192,64]{0,1:T(8,128)(2,1)} %param.12) | data formatting | bytes 2097152 | tf_op args[5]
  6.5 0.0 copy-done
  6.5 3.9 %copy.10 = bf16[8192,192]{1,0:T(8,128)(2,1)} copy(bf16[8192,192]{0,1:T(8,128)(2,1)S(1)} %copy-done) | data formatting | bytes 6291456 | tf_op args[1]
  10.4 77.7 %hyena_block.1 = (bf16[136,64]{1,0:T(8,128)(2,1)}, f32[4,128]{1,0:T(4,128)}, f32[1,64]{1,0:T(1,128)}) custom-call(bf16[136,64]{1,0:T(8,128)(2,1)} %copy.11.tok, bf16[136,64]{1,0:T(8,128)(2,1)} %copy.12.grd, bf16[4,32,64,192]{3,2,1,0:T(8,128)(2,1)} %bitcast.3, f32[3,192]{1,0:T(4,128)} %sfl.1, f32[4,128]{1,0:T(4,128)} %flt.1, f32[1,64]{1,0:T(1,128)} %bitcast.4, ...), custom_call_target="tpu_custom_call" | custom-call | tf_op jit(solution)/shard_map/hyena_block/pallas_call | solution.py:414
  88.0 1.5 %copy.14 = bf16[136,64]{0,1:T(8,128)(2,1)} copy(bf16[136,64]{1,0:T(8,128)(2,1)} %get-tuple-element.9) | data formatting | bytes 34816
  89.5 1.2 %copy.17 = f32[4,128]{1,0:T(4,128)} copy(f32[4,128]{1,0:T(4,128)} %get-tuple-element.16) | data formatting | bytes 4096
  90.8 1.2 %copy.18 = f32[64]{0:T(128)} copy(f32[64]{0:T(128)} %bitcast.5) | data formatting | bytes 512
Async XLA Ops:
  0.6 5.9 %copy-start = (bf16[8192,192]{0,1:T(8,128)(2,1)S(1)}, bf16[8192,192]{0,1:T(8,128)(2,1)}, u32[]{:S(2)}) copy-start(bf16[8192,192]{0,1:T(8,128)(2,1)} %param.8) | copy-start | bytes 9437188

commit v2 on v1

--- a/solution.py
+++ b/solution.py
@@ -96,9 +96,9 @@
 
 
 def kernel(
-    tok, grd, win, sfl, flt, skp, wout,
-    out_ref, fg_ref, sg_ref,
-    wv, wov, zr, gath, wpk, wrv, wz, acc, gz, gp, gr, yp, yr, hs, hr, pb, h2r, gated, op, orv, pr, toep,
+    tok_in, grd_in, win, sfl_in, flt_in, skp_in, wout,
+    res_ref,
+    tok, grd, sfl, flt, skp, wraw, wv, zr, gath, wz, acc, gz, gp, gr, yp, yr, hs, hr, pb, h2r, gated, op, orv, pr, toep,
     ss, rs, ls,
 ):
     r = lax.axis_index("row")
@@ -122,44 +122,36 @@
     sibling = (r + sgn, c)
     own = chunk(0, 0)
 
-    loads = [pltpu.make_async_copy(wout, wov, ls.at[0])]
-    for k in range(NZ):
-        loads.append(pltpu.make_async_copy(win.at[k], wv.at[:, pl.ds(64 * k, 64), :], ls.at[1 + k]))
-    for load in loads:
-        load.start()
-
     peers = [at(dz=i) for i in range(1, NZ)] + [at(dx=i) for i in range(1, NX)]
     peers += [at(dy=i) for i in range(1, NY)] + [by_row(i) for i in range(1, NR)]
     barrier = pltpu.get_barrier_semaphore()
     for peer in peers:
         pl.semaphore_signal(barrier, inc=1, device_id=peer, device_id_type=MESH)
 
-    both = jnp.concatenate([tok[...].astype(F32), grd[...].astype(F32)], 1)
-    zr[z] = jnp.concatenate([both, jnp.zeros((PAD - ROWS, 128), F32)], 0).astype(BF)
+    mine = pl.multiple_of(z * 2048, 2048)
+    keep = pl.multiple_of(z * 64, 64)
+    pairs = [(tok_in, tok), (grd_in, grd), (sfl_in, sfl), (flt_in, flt), (skp_in, skp), (win, wraw)]
+    pairs.append((wout.at[:, pl.ds(mine, 2048)], wz.at[pl.ds(keep, 64)]))
+    loads = [pltpu.make_async_copy(a, b, ls.at[i]) for i, (a, b) in enumerate(pairs)]
+    for load in loads:
+        load.start()
+    loads[0].wait()
+    loads[1].wait()
+    both = jnp.concatenate([tok[...].astype(F32), grd[...].astype(F32)], 0)
+    both = jnp.concatenate([both, jnp.zeros((128, 256 - ROWS), F32)], 1)
+    zr[z] = both.T[:PAD].astype(BF)
 
     pl.semaphore_wait(barrier, len(peers))
 
     z_moves = [comm.send(zr.at[z], zr.at[z], at(dz=i)) for i in (1, 2, 3)]
-
-    loads[0].wait()
-    half = pl.multiple_of(core * 512, 512)
-    w_moves = []
-    for i in (1, 2, 3):
-        base = pl.multiple_of(((z + i) % NZ) * 2048 + core * 512, 512)
-        a = wov[pl.ds(base, 512), :].astype(F32)
-        b = wov[pl.ds(base + 1024, 512), :].astype(F32)
-        wpk[i - 1] = jnp.concatenate([a, b], 1).astype(BF)
-        w_moves.append(comm.send(wpk.at[i - 1], wrv.at[z, pl.ds(half, 512)], at(dz=i)))
-    mine = pl.multiple_of(z * 2048, 2048)
-    wrv[z] = jnp.concatenate(
-        [wov[pl.ds(mine, 1024), :].astype(F32), wov[pl.ds(mine + 1024, 1024), :].astype(F32)], 1
-    ).astype(BF)
 
     col = iota((192, WIDE), 1)
     lane = col & 127
     source = (lane >> 4) * 48 + (col >> 7) * 16 + (lane & 15)
     hit = (iota((192, WIDE), 0) == source) & (lane < 64)
     perm = jnp.where(hit, 1.0, 0.0)
+    loads[2].wait()
+    loads[3].wait()
     short_taps = jnp.dot(sfl[...], perm, precision=HIGH, preferred_element_type=F32)
     perm_b = perm.astype(BF)
 
@@ -169,10 +161,26 @@
         line = jnp.broadcast_to(taps0[g : g + 1], (PAD, WIDE))
         toep[pl.ds(g * PAD, PAD)] = pltpu.roll(line, 0, 1, stride=1, stride_axis=0).astype(BF)
 
-    for load in loads[1:]:
-        load.wait()
+    loads[5].wait()
+
+    def reorder(pair, carry):
+        tiles = [wraw[:, pl.ds(pl.multiple_of(k * 2048 + pair * 128, 128), 128)] for k in range(NZ)]
+        t0, t1, t2, t3 = [v.astype(F32) for v in tiles]
+        wv[2 * pair] = jnp.concatenate([lows(t0, t1), lows(t2, t3)], 1).astype(BF)
+        wv[2 * pair + 1] = jnp.concatenate([highs(t0, t1), highs(t2, t3)], 1).astype(BF)
+        return carry
+
+    lax.fori_loop(0, NP // 2, reorder, 0)
     for i, move in zip((1, 2, 3), z_moves):
         comm.arrive(move, zr.at[(z - i + NZ) % NZ])
+    half = pl.multiple_of(core * 1024, 1024)
+    w_moves = []
+    for i in (1, 2, 3):
+        base = pl.multiple_of(((z + i) % NZ) * 2048 + core * 1024, 1024)
+        w_moves.append(
+            comm.send(wout.at[:, pl.ds(base, 1024)], wz.at[pl.ds(keep, 64), pl.ds(half, 1024)], at(dz=i))
+        )
+
     q0, q1, q2, q3 = [zr[k].astype(F32) for k in range(NZ)]
     gath[own] = jnp.concatenate([lows(q0, q1), lows(q2, q3)], 1).astype(BF)
     gz[...] = jnp.concatenate([highs(q0, q1), highs(q2, q3)], 1).astype(BF)
@@ -196,8 +204,7 @@
         if dx == 0:
             pass_on(part, 0, dy, 1, dy, 1, 0)
             pass_on(part, 0, dy, -1, dy, -1, 0)
-        if dx == -1:
-            pass_on(part, sgn, dy, 2, dy, sgn, 0)
+            pass_on(part, 0, dy, 2, dy, 2, 0)
 
     def forward(part, dx, dy):
         if part == "A":
@@ -209,9 +216,12 @@
                 x_steps(part, dx, 0)
             y_steps(part, dx, dy)
 
+    def hops(d):
+        return min(abs(d[0]), 1) + abs(d[1])
+
     order = sorted(
         [(dx, dy) for dx in (0, 1, -1, 2) for dy in (0, 1, -1, 2, -2, 3, -3, 4)],
-        key=lambda d: (abs(d[0]) + abs(d[1]), abs(d[0]), -d[0], -d[1]),
+        key=lambda d: (hops(d), abs(d[0]), -d[0], -d[1]),
     )
     forward("A", 0, 0)
     forward("B", 0, 0)
@@ -220,23 +230,37 @@
         total = None
         for dx, dy in places:
             p = chunk(dx, dy)
-            term = dot(gath[p], wv[p])
+            term = dot_t(gath[p], wv[p])
             total = term if total is None else total + term
         return total
 
     acc[...] = project([(0, 0)])
     w_back = []
-    for hop in range(1, 7):
-        places = [d for d in order if abs(d[0]) + abs(d[1]) == hop]
+    gx_moves = []
+
+    def sum_over_x():
+        loads[6].wait()
+        other = pl.multiple_of(1024 - core * 1024, 1024)
+        for i, move in zip((1, 2, 3), w_back):
+            comm.arrive(move, wz.at[pl.ds(pl.multiple_of(((z - i + NZ) % NZ) * 64, 64), 64), pl.ds(other, 1024)])
+        for k in range(NX):
+            gp[k] = dot(gz[...], wz[:, pl.ds(512 * k, 512)]).astype(BF)
+        for i in (1, 3, 2):
+            gx_moves.append(comm.send(gp.at[(x + i) % NX], gr.at[x], at(dx=i)))
+
+    for hop in range(1, 6):
+        places = [d for d in order if hops(d) == hop]
         for dx, dy in places:
             for part in ("A", "B"):
                 comm.arrive(moves[part, dx, dy], gath.at[chunk(dx, dy), parts[part]])
                 forward(part, dx, dy)
-        if hop == 4:
+        if hop == 3:
             for i, move in zip((1, 2, 3), w_moves):
-                ref = wrv.at[(z - i + NZ) % NZ, pl.ds(half, 512)]
+                ref = wz.at[pl.ds(pl.multiple_of(((z - i + NZ) % NZ) * 64, 64), 64), pl.ds(half, 1024)]
                 comm.arrive(move, ref)
                 w_back.append(comm.send(ref, ref, sibling))
+        if hop == 4:
+            sum_over_x()
         acc[...] += project(places)
 
     proj = dot(acc[...].astype(BF), perm_b)
@@ -251,22 +275,6 @@
     mixed = jnp.where(live, short[:, 128:256] * short[:, 256:384], 0.0)
     hs[...] = lows(mixed[8:72], mixed[72:136]).astype(BF)
     halo_move = comm.send(hs, hr, by_row(1))
-
-    other = pl.multiple_of(512 - core * 512, 512)
-    for i, move in zip((1, 2, 3), w_back):
-        comm.arrive(move, wrv.at[(z - i + NZ) % NZ, pl.ds(other, 512)])
-
-    def build(i, carry):
-        at_row = pl.multiple_of(i * 128, 128)
-        w0, w1, w2, w3 = [wrv[k, pl.ds(at_row, 128), :].astype(F32) for k in range(NZ)]
-        wz[pl.ds(at_row, 128), :] = jnp.concatenate([lows(w0, w1), lows(w2, w3)], 1).astype(BF)
-        wz[pl.ds(at_row + 1024, 128), :] = jnp.concatenate([highs(w0, w1), highs(w2, w3)], 1).astype(BF)
-        return carry
-
-    lax.fori_loop(0, 8, build, 0)
-    for k in range(NX):
-        gp[k] = dot_t(gz[...], wz[pl.ds(512 * k, 512), :]).astype(BF)
-    gx_moves = [comm.send(gp.at[(x + i) % NX], gr.at[x], at(dx=i)) for i in (1, 3, 2)]
 
     comm.arrive(tail_move, h2r)
     last = jnp.where(r > 0, h2r[...].astype(F32), 0.0)
@@ -287,6 +295,7 @@
     conv = jnp.zeros((PAD, 128), F32)
     for g in range(4):
         conv = jnp.where(group == g, big[g * PAD : (g + 1) * PAD], conv)
+    loads[4].wait()
     skip = jnp.concatenate([skp[...], jnp.zeros((1, 64), F32)], 1)
     value = query * (conv + skip * mixed)
     gated[own] = pack(value, 0).astype(BF)
@@ -360,7 +369,7 @@
         u0, u1, u2, u3 = [gated[4 * k + i].astype(F32) for i in range(4)]
         top = jnp.concatenate([lows(u0, u1), lows(u2, u3)], 1)
         rest = jnp.concatenate([highs(u0, u1), highs(u2, u3)], 1)[: PAD - CUT]
-        outp = outp + dot(jnp.concatenate([top, rest], 0).astype(BF), wz[pl.ds(256 * k, 256), :])
+        outp = outp + dot_t(jnp.concatenate([top, rest], 0).astype(BF), wz[:, pl.ds(256 * k, 256)])
     for k in range(NZ):
         op[k] = pack(outp[:, 128 * (k // 2) : 128 * (k // 2) + 128], k % 2).astype(BF)
     o_moves = [comm.send(op.at[(z + i) % NZ], orv.at[z], at(dz=i)) for i in (1, 2, 3)]
@@ -368,30 +377,39 @@
     for i, move in zip((1, 2, 3), o_moves):
         comm.arrive(move, orv.at[(z - i + NZ) % NZ])
         result = result + orv[(z - i + NZ) % NZ].astype(F32)
-    out_ref[...] = unpack(result)[:ROWS, :64].astype(BF)
+    res_ref[pl.ds(0, ROWS)] = unpack(result)[:ROWS]
 
     for i, move in zip(range(1, NR), row_moves):
         comm.arrive(move, pr.at[(r - i + NR) % NR])
     sums = pr[0]
     for k in range(1, NR):
         sums = sums + pr[k]
-    fg_ref[...] = sums[:4]
-    sg_ref[...] = sums[4:5, :64]
+    res_ref[pl.ds(ROWS, 8)] = sums
     comm.finish()
     assert comm.count <= NSEM
+
+
+def split_results(res_ref, out_ref, fg_ref, sg_ref):
+    block = jnp.concatenate([res_ref[pl.ds(0, ROWS)], jnp.zeros((256 - ROWS, 128), F32)], 0)
+    out_ref[...] = block.T[:64, :ROWS].astype(BF)
+    fg_ref[...] = res_ref[pl.ds(ROWS, 4)]
+    sg_ref[...] = res_ref[pl.ds(ROWS + 4, 1), pl.ds(0, 64)]
 
 
 def local(tokens, w_in, short_filter, mr_filter, skip, w_out, grad_out):
     vmem = pl.BlockSpec(memory_space=pltpu.VMEM)
     hbm = pl.BlockSpec(memory_space=pl.ANY)
     scratch = [
-        pltpu.VMEM((NP, 256, 192), BF),
-        pltpu.VMEM((8192, 64), BF),
+        pltpu.VMEM((64, ROWS), BF),
+        pltpu.VMEM((64, ROWS), BF),
+        pltpu.VMEM((3, 192), F32),
+        pltpu.VMEM((4, TAPS), F32),
+        pltpu.VMEM((1, 64), F32),
+        pltpu.VMEM((192, 8192), BF),
+        pltpu.VMEM((NP, 192, 256), BF),
         pltpu.VMEM((NZ, PAD, 128), BF),
         pltpu.VMEM((NP, PAD, 256), BF),
-        pltpu.VMEM((NZ - 1, 512, 128), BF),
-        pltpu.VMEM((NZ, 1024, 128), BF),
-        pltpu.VMEM((2048, 256), BF),
+        pltpu.VMEM((256, 2048), BF),
         pltpu.VMEM((PAD, 192), F32),
         pltpu.VMEM((PAD, 256), BF),
         pltpu.VMEM((NX, PAD, 512), BF),
@@ -409,24 +427,31 @@
         pltpu.VMEM((4 * PAD, WIDE), BF),
         pltpu.SemaphoreType.DMA((NSEM,)),
         pltpu.SemaphoreType.DMA((NSEM,)),
-        pltpu.SemaphoreType.DMA((1 + NZ,)),
+        pltpu.SemaphoreType.DMA((7,)),
     ]
-    out, taps, gains = pl.pallas_call(
+    sums = pl.pallas_call(
         kernel,
-        out_shape=(
-            jax.ShapeDtypeStruct((ROWS, 64), BF),
-            jax.ShapeDtypeStruct((4, TAPS), F32),
-            jax.ShapeDtypeStruct((1, 64), F32),
-        ),
-        in_specs=[vmem, vmem, hbm, vmem, vmem, vmem, hbm],
-        out_specs=(vmem, vmem, vmem),
+        out_shape=jax.ShapeDtypeStruct((PAD, 128), F32),
+        in_specs=[hbm] * 7,
+        out_specs=vmem,
         scratch_shapes=scratch,
         compiler_params=pltpu.CompilerParams(
             collective_id=0, has_side_effects=True, vmem_limit_bytes=56 * 1024 * 1024
         ),
         name="hyena_block",
-    )(tokens, grad_out, w_in.reshape(NZ, NP, 64, 192), short_filter, mr_filter, skip.reshape(1, 64), w_out)
-    return out, taps, gains.reshape(64)
+    )(tokens.T, grad_out.T, w_in.T, short_filter, mr_filter, skip.reshape(1, 64), w_out.T)
+    out, taps, gains = pl.pallas_call(
+        split_results,
+        out_shape=(
+            jax.ShapeDtypeStruct((64, ROWS), BF),
+            jax.ShapeDtypeStruct((4, TAPS), F32),
+            jax.ShapeDtypeStruct((1, 64), F32),
+        ),
+        in_specs=[vmem],
+        out_specs=(vmem, vmem, vmem),
+        name="split_results",
+    )(sums)
+    return out.T, taps, gains.reshape(64)
 
 
 def solution(mesh):

time: 92.8 us -> 72.6 us (0.78)
  local copies, waits for them, and re-layouts: 13.6 us -> 0 us
  Pallas kernels: 77.7 us -> 71.8 us
    unnamed x9 -> x0, local copies, waits for them, and re-layouts: 13.6 us -> none
    pallas_call x1 -> x2, Pallas kernels: 77.7 us -> 71.8 us  [the longest x1 70.2 us: local(): pl.pallas_call(kernel, out_shape=jax.ShapeDtypeStruct((PAD, 128), F32), i...]
where the time goes in v2:
time: 72.6 us; the launch traced here: 72.4 us
  Pallas kernels  71.8 us (99%)
    pallas_call x1, Pallas kernels, local(): pl.pallas_call(kernel, out_shape=jax.ShapeDtypeStruct((PAD, 128), F32), i...  70.2 us
    pallas_call x1, Pallas kernels, local(): pl.pallas_call(split_results, out_shape=(jax.ShapeDtypeStruct((64, ROWS),...  1.59 us

profile of v2, /device:TPU:1, one launch (start us, length us, event | category | flops | bytes accessed | tf_op | source)
XLA Modules:
  0.0 72.4 jit_solution(2829141899589130184)
XLA Ops:
  0.6 70.2 %hyena_block.1.res_ref = f32[144,128]{1,0:T(8,128)} custom-call(bf16[64,136]{1,0:T(8,128)(2,1)} %bitcast.9, bf16[64,136]{1,0:T(8,128)(2,1)} %bitcast.10, bf16[192,8192]{1,0:T(8,128)(2,1)} %bitcast.7, f32[3,192]{1,0:T(4,128)} %sfl_in.1, f32[4,128]{1,0:T(4,128)} %flt_in.1, f32[1,64]{1,0:T(1,128)} %bitcast.11, bf16[64,8192]{1,0:T(8,128)(2,1)} %bitcast.8), custom_call_target="tpu_custom_call" | custom-call | tf_op jit(solution)/shard_map/hyena_block/pallas_call | solution.py:432
  70.8 1.6 %split_results.1 = (bf16[64,136]{1,0:T(8,128)(2,1)}, f32[4,128]{1,0:T(4,128)}, f32[1,64]{1,0:T(1,128)}) custom-call(f32[144,128]{1,0:T(8,128)} %hyena_block.1.res_ref), custom_call_target="tpu_custom_call" | custom-call | tf_op jit(solution)/shard_map/split_results/pallas_call | solution.py:443

commit v3 on v2

--- a/solution.py
+++ b/solution.py
@@ -87,6 +87,13 @@
     return jnp.where(low(full), full, 0.0)
 
 
+def side_by_side(ref):
+    q0, q1, q2, q3 = [ref[k].astype(F32) for k in range(4)]
+    top = jnp.concatenate([lows(q0, q1), lows(q2, q3)], 1)
+    rest = jnp.concatenate([highs(q0, q1), highs(q2, q3)], 1)[: PAD - CUT]
+    return jnp.concatenate([top, rest], 0).astype(BF)
+
+
 def dot(a, b):
     return jnp.dot(a, b, preferred_element_type=F32)
 
@@ -98,7 +105,7 @@
 def kernel(
     tok_in, grd_in, win, sfl_in, flt_in, skp_in, wout,
     res_ref,
-    tok, grd, sfl, flt, skp, wraw, wv, zr, gath, wz, acc, gz, gp, gr, yp, yr, hs, hr, pb, h2r, gated, op, orv, pr, toep,
+    tok, grd, sfl, flt, skp, wraw, wv, zr, zg, gath, wz, acc, gz, gp, gr, yp, yr, hs, hr, pb, h2r, gated, op, orv, pr, toep,
     ss, rs, ls,
 ):
     r = lax.axis_index("row")
@@ -139,7 +146,9 @@
     loads[1].wait()
     both = jnp.concatenate([tok[...].astype(F32), grd[...].astype(F32)], 0)
     both = jnp.concatenate([both, jnp.zeros((128, 256 - ROWS), F32)], 1)
-    zr[z] = both.T[:PAD].astype(BF)
+    both = both.T[:PAD]
+    zr[z] = pack(both, 0).astype(BF)
+    zg[z] = pack(both, 1).astype(BF)
 
     pl.semaphore_wait(barrier, len(peers))
 
@@ -173,6 +182,8 @@
     lax.fori_loop(0, NP // 2, reorder, 0)
     for i, move in zip((1, 2, 3), z_moves):
         comm.arrive(move, zr.at[(z - i + NZ) % NZ])
+    g_moves = [comm.send(zg.at[z], zg.at[z], at(dz=i)) for i in (1, 2, 3)]
+
     half = pl.multiple_of(core * 1024, 1024)
     w_moves = []
     for i in (1, 2, 3):
@@ -181,9 +192,7 @@
             comm.send(wout.at[:, pl.ds(base, 1024)], wz.at[pl.ds(keep, 64), pl.ds(half, 1024)], at(dz=i))
         )
 
-    q0, q1, q2, q3 = [zr[k].astype(F32) for k in range(NZ)]
-    gath[own] = jnp.concatenate([lows(q0, q1), lows(q2, q3)], 1).astype(BF)
-    gz[...] = jnp.concatenate([highs(q0, q1), highs(q2, q3)], 1).astype(BF)
+    gath[own] = side_by_side(zr)
 
     parts = {"A": pl.ds(0, CUT), "B": pl.ds(CUT, PAD - CUT)}
     moves = {}
@@ -243,6 +252,9 @@
         other = pl.multiple_of(1024 - core * 1024, 1024)
         for i, move in zip((1, 2, 3), w_back):
             comm.arrive(move, wz.at[pl.ds(pl.multiple_of(((z - i + NZ) % NZ) * 64, 64), 64), pl.ds(other, 1024)])
+        for i, move in zip((1, 2, 3), g_moves):
+            comm.arrive(move, zg.at[(z - i + NZ) % NZ])
+        gz[...] = side_by_side(zg)
         for k in range(NX):
             gp[k] = dot(gz[...], wz[:, pl.ds(512 * k, 512)]).astype(BF)
         for i in (1, 3, 2):
@@ -407,7 +419,8 @@
         pltpu.VMEM((1, 64), F32),
         pltpu.VMEM((192, 8192), BF),
         pltpu.VMEM((NP, 192, 256), BF),
-        pltpu.VMEM((NZ, PAD, 128), BF),
+        pltpu.VMEM((NZ, CUT, 128), BF),
+        pltpu.VMEM((NZ, CUT, 128), BF),
         pltpu.VMEM((NP, PAD, 256), BF),
         pltpu.VMEM((256, 2048), BF),
         pltpu.VMEM((PAD, 192), F32),

time: 72.6 us -> 71.4 us (0.983)
  Pallas kernels: 71.8 us -> 70.6 us
    pallas_call x1, Pallas kernels: 70.2 us -> 69 us  [local(): pl.pallas_call(kernel, out_shape=jax.ShapeDtypeStruct((PAD, 128), F32), i...]
where the time goes in v3:
time: 71.4 us; the launch traced here: 71.2 us
  Pallas kernels  70.6 us (99%)
    pallas_call x1, Pallas kernels, local(): pl.pallas_call(kernel, out_shape=jax.ShapeDtypeStruct((PAD, 128), F32), i...  69 us
    pallas_call x1, Pallas kernels, local(): pl.pallas_call(split_results, out_shape=(jax.ShapeDtypeStruct((64, ROWS),...  1.59 us

profile of v3, /device:TPU:1, one launch (start us, length us, event | category | flops | bytes accessed | tf_op | source)
XLA Modules:
  0.0 71.2 jit_solution(18422514279864151160)
XLA Ops:
  0.6 69.0 %hyena_block.1.res_ref = f32[144,128]{1,0:T(8,128)} custom-call(bf16[64,136]{1,0:T(8,128)(2,1)} %bitcast.9, bf16[64,136]{1,0:T(8,128)(2,1)} %bitcast.10, bf16[192,8192]{1,0:T(8,128)(2,1)} %bitcast.7, f32[3,192]{1,0:T(4,128)} %sfl_in.1, f32[4,128]{1,0:T(4,128)} %flt_in.1, f32[1,64]{1,0:T(1,128)} %bitcast.11, bf16[64,8192]{1,0:T(8,128)(2,1)} %bitcast.8), custom_call_target="tpu_custom_call" | custom-call | tf_op jit(solution)/shard_map/hyena_block/pallas_call | solution.py:445
  69.6 1.6 %split_results.1 = (bf16[64,136]{1,0:T(8,128)(2,1)}, f32[4,128]{1,0:T(4,128)}, f32[1,64]{1,0:T(1,128)}) custom-call(f32[144,128]{1,0:T(8,128)} %hyena_block.1.res_ref), custom_call_target="tpu_custom_call" | custom-call | tf_op jit(solution)/shard_map/split_results/pallas_call | solution.py:456

commit v4 on v3

--- a/solution.py
+++ b/solution.py
@@ -12,6 +12,7 @@
 PAD = 144
 CUT = 80
 CUT2 = 64
+REST = ROWS - CUT
 TAPS = 128
 WIDE = 384
 BF = jnp.bfloat16
@@ -91,7 +92,7 @@
     q0, q1, q2, q3 = [ref[k].astype(F32) for k in range(4)]
     top = jnp.concatenate([lows(q0, q1), lows(q2, q3)], 1)
     rest = jnp.concatenate([highs(q0, q1), highs(q2, q3)], 1)[: PAD - CUT]
-    return jnp.concatenate([top, rest], 0).astype(BF)
+    return jnp.concatenate([top, rest], 0)
 
 
 def dot(a, b):
@@ -105,7 +106,7 @@
 def kernel(
     tok_in, grd_in, win, sfl_in, flt_in, skp_in, wout,
     res_ref,
-    tok, grd, sfl, flt, skp, wraw, wv, zr, zg, gath, wz, acc, gz, gp, gr, yp, yr, hs, hr, pb, h2r, gated, op, orv, pr, toep,
+    tok, grd, sfl, flt, skp, wraw, wv, zr, zg, gath_a, gath_b, wz, acc, gz, gp, gr, yp, yr, hs, hr, pb, h2r, gated, op, orv, pr, toep,
     ss, rs, ls,
 ):
     r = lax.axis_index("row")
@@ -192,13 +193,15 @@
             comm.send(wout.at[:, pl.ds(base, 1024)], wz.at[pl.ds(keep, 64), pl.ds(half, 1024)], at(dz=i))
         )
 
-    gath[own] = side_by_side(zr)
-
-    parts = {"A": pl.ds(0, CUT), "B": pl.ds(CUT, PAD - CUT)}
+    mine_all = side_by_side(zr)
+    gath_a[own] = mine_all[:CUT].astype(BF)
+    gath_b[own] = jnp.concatenate([mine_all[CUT:ROWS, :128], mine_all[CUT:ROWS, 128:]], 0).astype(BF)
+
+    parts = {"A": gath_a, "B": gath_b}
     moves = {}
 
     def pass_on(part, dx, dy, to_dx, to_dy, step_x, step_y):
-        ref = gath.at[chunk(dx, dy), parts[part]]
+        ref = parts[part].at[chunk(dx, dy)]
         moves[part, to_dx, to_dy] = comm.send(ref, ref, at(dx=step_x, dy=step_y))
 
     def y_steps(part, dx, dy):
@@ -239,7 +242,8 @@
         total = None
         for dx, dy in places:
             p = chunk(dx, dy)
-            term = dot_t(gath[p], wv[p])
+            w, b = wv[p], gath_b[p]
+            term = jnp.concatenate([dot_t(gath_a[p], w), dot_t(b, w[:, :128]), dot_t(b, w[:, 128:])], 0)
             total = term if total is None else total + term
         return total
 
@@ -254,7 +258,7 @@
             comm.arrive(move, wz.at[pl.ds(pl.multiple_of(((z - i + NZ) % NZ) * 64, 64), 64), pl.ds(other, 1024)])
         for i, move in zip((1, 2, 3), g_moves):
             comm.arrive(move, zg.at[(z - i + NZ) % NZ])
-        gz[...] = side_by_side(zg)
+        gz[...] = side_by_side(zg).astype(BF)
         for k in range(NX):
             gp[k] = dot(gz[...], wz[:, pl.ds(512 * k, 512)]).astype(BF)
         for i in (1, 3, 2):
@@ -264,7 +268,7 @@
         places = [d for d in order if hops(d) == hop]
         for dx, dy in places:
             for part in ("A", "B"):
-                comm.arrive(moves[part, dx, dy], gath.at[chunk(dx, dy), parts[part]])
+                comm.arrive(moves[part, dx, dy], parts[part].at[chunk(dx, dy)])
                 forward(part, dx, dy)
         if hop == 3:
             for i, move in zip((1, 2, 3), w_moves):
@@ -275,7 +279,9 @@
             sum_over_x()
         acc[...] += project(places)
 
-    proj = dot(acc[...].astype(BF), perm_b)
+    rest = acc[pl.ds(CUT, REST)] + acc[pl.ds(CUT + 3 * REST, REST)]
+    whole = jnp.concatenate([acc[pl.ds(0, CUT)], rest, jnp.zeros((PAD - ROWS, 192), F32)], 0)
+    proj = dot(whole.astype(BF), perm_b)
     pb[...] = proj.astype(BF)
     tail_move = comm.send(pb.at[pl.ds(128, 16)], h2r, by_row(1))
     t = iota((PAD, WIDE), 0)
@@ -421,9 +427,10 @@
         pltpu.VMEM((NP, 192, 256), BF),
         pltpu.VMEM((NZ, CUT, 128), BF),
         pltpu.VMEM((NZ, CUT, 128), BF),
-        pltpu.VMEM((NP, PAD, 256), BF),
+        pltpu.VMEM((NP, CUT, 256), BF),
+        pltpu.VMEM((NP, 2 * REST, 128), BF),
         pltpu.VMEM((256, 2048), BF),
-        pltpu.VMEM((PAD, 192), F32),
+        pltpu.VMEM((CUT + 4 * REST, 192), F32),
         pltpu.VMEM((PAD, 256), BF),
         pltpu.VMEM((NX, PAD, 512), BF),
         pltpu.VMEM((NX, PAD, 512), BF),

time: 71.4 us -> 71.5 us (level)
  no operation moved by 1% of the time
where the time goes in v4:
time: 71.5 us; the launch traced here: 71.3 us
  Pallas kernels  70.6 us (99%)
    pallas_call x1, Pallas kernels, local(): pl.pallas_call(kernel, out_shape=jax.ShapeDtypeStruct((PAD, 128), F32), i...  69.1 us
    pallas_call x1, Pallas kernels, local(): pl.pallas_call(split_results, out_shape=(jax.ShapeDtypeStruct((64, ROWS),...  1.59 us

profile of v4, /device:TPU:1, one launch (start us, length us, event | category | flops | bytes accessed | tf_op | source)
XLA Modules:
  0.0 71.3 jit_solution(16246037827474157804)
XLA Ops:
  0.6 69.1 %hyena_block.1.res_ref = f32[144,128]{1,0:T(8,128)} custom-call(bf16[64,136]{1,0:T(8,128)(2,1)} %bitcast.9, bf16[64,136]{1,0:T(8,128)(2,1)} %bitcast.10, bf16[192,8192]{1,0:T(8,128)(2,1)} %bitcast.7, f32[3,192]{1,0:T(4,128)} %sfl_in.1, f32[4,128]{1,0:T(4,128)} %flt_in.1, f32[1,64]{1,0:T(1,128)} %bitcast.11, bf16[64,8192]{1,0:T(8,128)(2,1)} %bitcast.8), custom_call_target="tpu_custom_call" | custom-call | tf_op jit(solution)/shard_map/hyena_block/pallas_call | solution.py:452
  69.7 1.6 %split_results.1 = (bf16[64,136]{1,0:T(8,128)(2,1)}, f32[4,128]{1,0:T(4,128)}, f32[1,64]{1,0:T(1,128)}) custom-call(f32[144,128]{1,0:T(8,128)} %hyena_block.1.res_ref), custom_call_target="tpu_custom_call" | custom-call | tf_op jit(solution)/shard_map/split_results/pallas_call | solution.py:463
